TPU v7x, 32 devices: a whole 2x2x4 slice. The times are simulated.
32 devices in a mesh: blk: 8 (over y, x, core), exp: 4 (over z).
Axes of the slice: x: 2, y: 2, z: 4, core: 2. Of those that a mesh axis runs over, the one named last changes fastest.
Arguments:
- residual_deposit_sequence: bfloat16 [4, 1024, 1536], P('exp', 'blk'), may hold values from -60 to 60
- premix_rescaler: float32 [1536], replicated, may hold values from 0.25 to 1.75
- asking_projector: bfloat16 [1536, 1536], P(None, 'exp'), may hold values from -0.15625 to 0.15625
- lookup_projector: bfloat16 [1536, 512], P(None, 'exp'), may hold values from -0.15625 to 0.15625
- content_projector: bfloat16 [1536, 512], P(None, 'exp'), may hold values from -0.15625 to 0.15625
- final_projector: bfloat16 [1536, 1536], P('exp'), may hold values from -0.15625 to 0.15625
- logit_multipliers: float32 [12], replicated, may hold values from 1.5 to 6
- premixture_rescaler: float32 [1536], replicated, may hold values from 0.25 to 1.75
- specialist_switch_tensor: bfloat16 [8, 1536, 384], P('exp'), may hold values from -0.15625 to 0.15625
- specialist_widen_tensor: bfloat16 [8, 1536, 384], P('exp'), may hold values from -0.15625 to 0.15625
- specialist_shrink_tensor: bfloat16 [8, 384, 1536], P('exp'), may hold values from -0.3125 to 0.3125
- picked_specialist_labels: int32 [4, 1024, 2], P(None, 'blk'), may hold values from 0 to 7, all different within a row; in each aligned block of 128 rows (0 to 127, 128 to 255, ..., all dimensions but the last counted through in order) at most 64 rows name the same one
- specialist_shares: float32 [4, 1024, 2], P(None, 'blk'), may hold values from 0.1 to 1
Outputs:
- attention_update: bfloat16 [4, 1024, 1536], P('exp', 'blk')
- expert_update: bfloat16 [4, 1024, 1536], P('exp', 'blk')
Inputs may be any that keep to these rules, and one draw needn't show every extreme that they name: `picked_specialist_labels`: the 2 ids of a hit differ. Within each event's 128 hits on one index of blk (an aligned block of 128 rows) no expert is named by more than 64 hits, a bound that some block reaches.
All inputs are finite; a program needn't handle non-finite values.
Results may differ from a plain program's by a relative error of at most 0.019.
Values may be sent and summed in bfloat16 or wider, within the bound.
A program may use at most 192 MiB of HBM per device.

v0:
```python
import math
import jax
import jax.numpy as jnp
from jax import lax
from jax.sharding import PartitionSpec as P

D = 1536
PER_LANE_DIM = 128
TOP = 2
CAP = 64


def norm_rows(values, norm_gain):
    widened = values.astype(jnp.float32)
    return (
        widened * lax.rsqrt(jnp.mean(widened * widened, axis=-1, keepdims=True) + 1e-05) * norm_gain
    )


def head_norm(values):
    return values * lax.rsqrt(jnp.mean(values * values, axis=-1, keepdims=True) + 1e-06)


def attend_hits(
    rescaled_entries,
    asking_projector,
    lookup_projector,
    content_projector,
    final_projector,
    logit_multipliers,
):
    events, row_count, model_width = rescaled_entries.shape
    common_key_heads = lookup_projector.shape[1] // PER_LANE_DIM
    local_lane_count = asking_projector.shape[1] // PER_LANE_DIM
    askers_per_lookup = local_lane_count // common_key_heads
    query_heads = jnp.einsum(
        "std,de->ste", rescaled_entries, asking_projector, preferred_element_type=jnp.float32
    )
    query_heads = head_norm(
        query_heads.reshape(events, row_count, common_key_heads, askers_per_lookup, PER_LANE_DIM)
    ).astype(jnp.bfloat16)
    key_heads = jnp.einsum(
        "std,de->ste", rescaled_entries, lookup_projector, preferred_element_type=jnp.float32
    )
    key_heads = head_norm(
        key_heads.reshape(events, row_count, common_key_heads, PER_LANE_DIM)
    ).astype(jnp.bfloat16)
    value_heads = jnp.einsum(
        "std,de->ste", rescaled_entries, content_projector, preferred_element_type=jnp.float32
    )
    value_heads = value_heads.reshape(events, row_count, common_key_heads, PER_LANE_DIM).astype(
        jnp.bfloat16
    )
    inverse_root_dim = (logit_multipliers / math.sqrt(PER_LANE_DIM)).reshape(
        common_key_heads, askers_per_lookup
    )
    key_piece = lax.all_gather(key_heads, "blk", axis=1, tiled=True)
    value_piece = lax.all_gather(value_heads, "blk", axis=1, tiled=True)
    scores = jnp.einsum(
        "sikgd,sjkd->skgij", query_heads, key_piece, preferred_element_type=jnp.float32
    )
    expo = jnp.exp(scores * inverse_root_dim[None, :, :, None, None])
    totals = jnp.sum(expo, axis=-1)
    mixture = jnp.einsum(
        "skgij,sjkd->skgid",
        expo.astype(jnp.bfloat16),
        value_piece,
        preferred_element_type=jnp.float32,
    )
    totals, mixture = (totals, mixture)
    heads_out = head_norm(mixture / totals[..., None]).astype(jnp.bfloat16)
    out_blocks = final_projector.reshape(
        common_key_heads, askers_per_lookup, PER_LANE_DIM, model_width
    )
    return jnp.einsum("skgid,kgde->sie", heads_out, out_blocks, preferred_element_type=jnp.float32)


def gates_of(labels, shares, expert_ids):
    hit = labels[..., None, :] == expert_ids[:, None]
    return jnp.sum(jnp.where(hit, shares[..., None, :], 0.0), axis=-1)


def run_experts(rows, gates, switch, widen, shrink):
    gate_act = jnp.einsum("td,jdf->tjf", rows, switch, preferred_element_type=jnp.float32)
    up_act = jnp.einsum("td,jdf->tjf", rows, widen, preferred_element_type=jnp.float32)
    hidden = (jax.nn.silu(gate_act) * up_act * gates[:, :, None]).astype(jnp.bfloat16)
    return jnp.einsum("tjf,jfd->td", hidden, shrink, preferred_element_type=jnp.float32)


def body(
    residual_deposit_sequence,
    premix_rescaler,
    asking_projector,
    lookup_projector,
    content_projector,
    final_projector,
    logit_multipliers,
    premixture_rescaler,
    specialist_switch_tensor,
    specialist_widen_tensor,
    specialist_shrink_tensor,
    picked_specialist_labels,
    specialist_shares,
):
    specialist_slot = lax.axis_index("exp")
    exp_count = lax.axis_size("exp")
    rows_all = lax.all_gather(residual_deposit_sequence, "exp", axis=0, tiled=True)
    rescaled_entries = norm_rows(rows_all, premix_rescaler).astype(jnp.bfloat16)
    local_lane_count = asking_projector.shape[1] // PER_LANE_DIM
    device_scratch = lax.dynamic_slice_in_dim(
        logit_multipliers, specialist_slot * local_lane_count, local_lane_count
    )
    partial_out = attend_hits(
        rescaled_entries,
        asking_projector,
        lookup_projector,
        content_projector,
        final_projector,
        device_scratch,
    )
    attention_full = lax.psum_scatter(
        partial_out.astype(jnp.bfloat16), "exp", scatter_dimension=0, tiled=True
    ).astype(jnp.float32)
    attention_update = attention_full.astype(jnp.bfloat16)
    residual = residual_deposit_sequence.astype(jnp.float32) + attention_full
    expert_in = norm_rows(residual, premixture_rescaler).astype(jnp.bfloat16)
    local_experts = specialist_switch_tensor.shape[0]
    expert_ids = specialist_slot * local_experts + jnp.arange(local_experts, dtype=jnp.int32)
    gates = gates_of(picked_specialist_labels, specialist_shares, expert_ids)
    rows = lax.all_gather(expert_in, "exp", axis=0, tiled=True)
    events, row_count, _ = rows.shape
    summed = run_experts(
        rows.reshape(events * row_count, D),
        gates.reshape(events * row_count, local_experts),
        specialist_switch_tensor,
        specialist_widen_tensor,
        specialist_shrink_tensor,
    ).astype(jnp.bfloat16)
    expert_update = lax.psum_scatter(
        summed.reshape(events, row_count, D), "exp", scatter_dimension=0, tiled=True
    )
    return (attention_update, expert_update)


def solution(mesh):
    placed = (
        P("exp", "blk", None),
        P(),
        P(None, "exp"),
        P(None, "exp"),
        P(None, "exp"),
        P("exp", None),
        P(),
        P(),
        P("exp", None, None),
        P("exp", None, None),
        P("exp", None, None),
        P(None, "blk", None),
        P(None, "blk", None),
    )
    return jax.shard_map(
        body,
        mesh=mesh,
        in_specs=placed,
        out_specs=(P("exp", "blk", None), P("exp", "blk", None)),
        check_vma=False,
    )
```

profile of v0, /device:TPU:0, one launch (start us, length us, event | category | flops | bytes accessed | tf_op | source)
XLA Modules:
  0.0 236.5 jit_solution(15688548943295369664)
XLA Ops:
  7.2 0.0 copy-start
  7.2 0.0 copy-start.7
  7.2 0.0 all-gather.7.cloned.1.call-start
  7.2 0.7 all-gather.7.cloned.1.call-update
  7.9 0.0 all-gather.11.cloned.1.call-start
  8.0 41.4 %all-gather.7.cloned.1.call-done = bf16[4,128,1536]{2,1,0:T(8,128)(2,1)} async-done(((bf16[1,128,1536]{2,1,0:T(8,128)(2,1)}), bf16[4,128,1536]{2,1,0:T(8,128)(2,1)}) %all-gather.7.cloned.1.call-update) | async-done | bytes 1572880 | tf_op jit(solution)/shard_map/all_gather | solution.py:107
  49.4 0.0 copy-start.2
  49.4 1.9 fusion.1
  51.3 0.0 copy-done.7
  51.3 0.0 copy-done.2
  51.4 0.0 copy-start.8
  51.4 0.0 copy-start.9
  51.4 1.5 multiply_reduce_fusion.2
  52.9 0.7 multiply_convert_fusion.6
  53.6 0.0 all-gather.11.cloned.1.call-update
  53.6 0.0 copy-start.10
  53.6 0.0 all-gather.13.cloned.1.call-start
  53.7 0.0 copy-done.8
  53.7 0.0 copy-done.9
  53.7 2.7 %convolution_convert_fusion = bf16[4,128,128]{2,1,0:T(8,128)(2,1)} fusion(bf16[4,128,1536]{2,1,0:T(8,128)(2,1)} %all-gather.7.cloned.1.call-done, f32[1536]{0:T(1024)S(1)} %copy-done.9, f32[4,128]{1,0:T(4,128)S(1)} %add_rsqrt_fusion.3, bf16[1536,128]{1,0:T(8,128)(2,1)S(1)} %copy-done.8), kind=kOutput, calls=%fused_computation.19 | convolution fusion | flops 204537856 | bytes 2105344 | tf_op jit(solution)/shard_map/std,de->ste/dot_general | solution.py:48
  56.4 0.0 all-gather.13.cloned.1.call-update
  56.4 0.0 reduce-scatter.3.cloned.1.call-start
  56.5 0.0 copy-done.10
  56.5 0.1 dynamic-slice_multiply_fusion
  56.6 3.7 %fusion.31 = (f32[4,128,384]{2,1,0:T(8,128)S(1)}, f32[4,128,384]{2,1,0:T(8,128)}) fusion(bf16[1536,384]{1,0:T(8,128)(2,1)} %param.15, bf16[4,128,1536]{2,1,0:T(8,128)(2,1)} %all-gather.7.cloned.1.call-done, f32[1536]{0:T(1024)S(1)} %copy-done.9, f32[4,128]{1,0:T(4,128)S(1)} %add_rsqrt_fusion.3), kind=kOutput, calls=%fused_computation.49 | convolution fusion | flops 607322112 | bytes 4333568 | tf_op jit(solution)/shard_map/std,de->ste/dot_general | solution.py:36
  60.2 1.2 copy.43
  61.4 1.4 copy.42
  62.8 1.2 reduce_sum.65
  64.0 12.2 %all-gather.11.cloned.1.call-done = bf16[4,1024,128]{1,2,0:T(8,128)(2,1)} async-done(((bf16[4,128,128]{1,2,0:T(8,128)(2,1)}), bf16[4,1024,128]{1,2,0:T(8,128)(2,1)}) %all-gather.11.cloned.1.call-update) | async-done | bytes 1048592 | tf_op jit(solution)/shard_map/all_gather | solution.py:57
  76.2 5.4 %bitcast_reduce_fusion = (f32[4,3,128]{2,1,0:T(4,128)S(1)}, f32[4,1024,128,3]{2,1,3,0:T(8,128)}) fusion(f32[3]{0:T(128)S(1)} %dynamic-slice_multiply_fusion, f32[4,128,3,128]{1,3,2,0:T(8,128)S(1)} %bitcast.91, f32[4,128,3]{1,2,0:T(4,128)S(1)} %add_rsqrt_fusion.1, bf16[4,1024,128]{1,2,0:T(8,128)(2,1)} %all-gather.11.cloned.1.call-done), kind=kOutput, calls=%fused_computation | convolution fusion | flops 406190592 | bytes 8138764 | tf_op jit(solution)/shard_map/sikgd,sjkd->skgij/dot_general | solution.py:59
  81.6 20.6 %all-gather.13.cloned.1.call-done = bf16[4,1024,128]{2,1,0:T(8,128)(2,1)} async-done(((bf16[4,128,128]{2,1,0:T(8,128)(2,1)}), bf16[4,1024,128]{2,1,0:T(8,128)(2,1)}) %all-gather.13.cloned.1.call-update) | async-done | bytes 1048592 | tf_op jit(solution)/shard_map/all_gather | solution.py:58
  102.2 0.0 copy-start.3
  102.2 4.4 %multiply_reduce_fusion.1 = (f32[4,3,128]{2,1,0:T(4,128)S(1)}, f32[4,3,128,128]{2,3,1,0:T(8,128)S(1)}) fusion(f32[4,3,128]{2,1,0:T(4,128)S(1)} %get-tuple-element.6, bf16[4,1024,128]{2,1,0:T(8,128)(2,1)} %all-gather.13.cloned.1.call-done, f32[4,1024,128,3]{2,1,3,0:T(8,128)} %get-tuple-element.7, f32[3]{0:T(128)S(1)} %dynamic-slice_multiply_fusion), kind=kOutput, calls=%fused_computation.31 | convolution fusion | flops 406387200 | bytes 8138764 | tf_op jit(solution)/shard_map/skgij,sjkd->skgid/dot_general | solution.py:64
  106.7 0.0 copy-done.3
  106.7 2.2 fusion.8
  108.9 0.0 copy-start.1
  108.9 0.0 copy-start.4
  108.9 0.0 reduce-scatter.3.cloned.1.call-update
  108.9 0.0 copy-start.5
  108.9 0.0 copy-start.6
  108.9 0.0 all-gather.9.cloned.1.call-start
  109.0 35.4 %reduce-scatter.3.cloned.1.call-done = bf16[1,128,1536]{2,1,0:T(8,128)(2,1)} async-done(((bf16[4,128,1536]{2,1,0:T(8,128)(2,1)}), bf16[1,128,1536]{2,1,0:T(8,128)(2,1)}) %reduce-scatter.3.cloned.1.call-update) | async-done | bytes 393232 | tf_op jit(solution)/shard_map/reduce_scatter | solution.py:121
  144.4 0.0 copy-done.1
  144.4 1.2 multiply_reduce_fusion
  145.6 0.0 copy-done.4
  145.6 1.9 multiply_convert_fusion.1
  147.5 0.0 all-gather.9.cloned.1.call-update
  147.5 0.0 reduce-scatter.5.cloned.1.call-start
  147.6 0.0 copy-done.5
  147.6 0.0 copy-done.6
  147.6 0.1 select_reduce_fusion
  147.7 36.0 %all-gather.9.cloned.1.call-done = bf16[4,128,1536]{2,1,0:T(8,128)(2,1)} async-done(((bf16[1,128,1536]{2,1,0:T(8,128)(2,1)}), bf16[4,128,1536]{2,1,0:T(8,128)(2,1)}) %all-gather.9.cloned.1.call-update) | async-done | bytes 1572880 | tf_op jit(solution)/shard_map/all_gather | solution.py:130
  183.7 4.7 %fusion.32 = f32[512,2,384]{2,0,1:T(8,128)} fusion(bf16[512,1536,1]{1,0,2:T(8,128)(2,1)} %bitcast.97, bf16[2,1536,384]{2,1,0:T(8,128)(2,1)} %param.21), kind=kOutput, calls=%fused_computation.50 | convolution fusion | flops 1207959552 | bytes 5505024 | tf_op jit(solution)/shard_map/td,jdf->tjf/dot_general | solution.py:84
  188.4 0.0 copy-done
  188.4 6.9 %fusion.9 = bf16[512,1536]{1,0:T(8,128)(2,1)} fusion(bf16[2,384,1536]{2,1,0:T(8,128)(2,1)S(1)} %copy-done, f32[512,2,384]{2,0,1:T(8,128)} %fusion.32, bf16[512,1536,1]{1,0,2:T(8,128)(2,1)} %bitcast.98, bf16[2,1536,384]{2,1,0:T(8,128)(2,1)} %param.22, f32[512,2]{0,1:T(2,128)S(1)} %bitcast.96), kind=kOutput, calls=%fused_computation.15 | convolution fusion | flops 2419458048 | bytes 9441280 | tf_op jit(solution)/shard_map/tjf,jfd->td/dot_general | solution.py:87
  195.3 0.0 reduce-scatter.5.cloned.1.call-update
  195.3 34.3 %reduce-scatter.5.cloned.1.call-done = bf16[1,128,1536]{2,1,0:T(8,128)(2,1)} async-done(((bf16[4,128,1536]{2,1,0:T(8,128)(2,1)}), bf16[1,128,1536]{2,1,0:T(8,128)(2,1)}) %reduce-scatter.5.cloned.1.call-update) | async-done | bytes 393232 | tf_op jit(solution)/shard_map/reduce_scatter | solution.py:139
  (9 shorter events, 0.1 us)
Async XLA Ops:
  7.2 181.2 %copy-start = (bf16[2,384,1536]{2,1,0:T(8,128)(2,1)S(1)}, bf16[2,384,1536]{2,1,0:T(8,128)(2,1)}, u32[]{:S(2)}) copy-start(bf16[2,384,1536]{2,1,0:T(8,128)(2,1)} %param.23) | copy-start | bytes 7077892
  7.2 44.2 %copy-start.7 = (bf16[1536,128]{1,0:T(8,128)(2,1)S(1)}, bf16[1536,128]{1,0:T(8,128)(2,1)}, u32[]{:S(2)}) copy-start(bf16[1536,128]{1,0:T(8,128)(2,1)} %param.16) | copy-start | bytes 1179652
  7.2 42.2 %all-gather.7.cloned.1.call-start = ((), (), s32[]{:S(2)}) async-start(), calls=%async_computation.2 | async-start | bytes 1966080 | tf_op jit(solution)/shard_map/all_gather | solution.py:107
  7.9 68.3 %all-gather.11.cloned.1.call-start = ((), (), s32[]{:S(2)}) async-start(), calls=%async_computation.6 | async-start | bytes 1179648 | tf_op jit(solution)/shard_map/all_gather | solution.py:57
  49.4 1.9 copy-start.2
  51.4 2.3 copy-start.8
  51.4 2.3 copy-start.9
  53.6 2.9 %copy-start.10 = (f32[12]{0:T(128)S(1)}, f32[12]{0:T(128)}, u32[]{:S(2)}) copy-start(f32[12]{0:T(128)} %param.19) | copy-start | bytes 148
  53.6 48.6 %all-gather.13.cloned.1.call-start = ((), (), s32[]{:S(2)}) async-start(), calls=%async_computation.7 | async-start | bytes 1179648 | tf_op jit(solution)/shard_map/all_gather | solution.py:58
  56.4 87.9 %reduce-scatter.3.cloned.1.call-start = ((), (), s32[]{:S(2)}) async-start(), calls=%async_computation.3 | async-start | bytes 1966080 | tf_op jit(solution)/shard_map/reduce_scatter | solution.py:121
  102.2 4.5 %copy-start.3 = (bf16[384,1536]{1,0:T(8,128)(2,1)S(1)}, bf16[384,1536]{1,0:T(8,128)(2,1)}, u32[]{:S(2)}) copy-start(bf16[384,1536]{1,0:T(8,128)(2,1)} %param.18) | copy-start | bytes 3538948
  108.9 35.5 %copy-start.1 = (bf16[1,128,1536]{2,1,0:T(8,128)(2,1)S(1)}, bf16[1,128,1536]{2,1,0:T(8,128)(2,1)}, u32[]{:S(2)}) copy-start(bf16[1,128,1536]{2,1,0:T(8,128)(2,1)} %param.13) | copy-start | bytes 1179652
  108.9 36.7 %copy-start.4 = (f32[1536]{0:T(1024)S(1)}, f32[1536]{0:T(1024)}, u32[]{:S(2)}) copy-start(f32[1536]{0:T(1024)} %param.20) | copy-start | bytes 18436
  108.9 38.6 %copy-start.5 = (s32[4,128,2]{1,2,0:T(2,128)S(1)}, s32[4,128,2]{1,2,0:T(2,128)}, u32[]{:S(2)}) copy-start(s32[4,128,2]{1,2,0:T(2,128)} %param.24) | copy-start | bytes 12292
  108.9 38.7 %copy-start.6 = (f32[4,128,2]{1,2,0:T(2,128)S(1)}, f32[4,128,2]{1,2,0:T(2,128)}, u32[]{:S(2)}) copy-start(f32[4,128,2]{1,2,0:T(2,128)} %param.25) | copy-start | bytes 12292
  108.9 74.8 %all-gather.9.cloned.1.call-start = ((), (), s32[]{:S(2)}) async-start(), calls=%async_computation.4 | async-start | bytes 1966080 | tf_op jit(solution)/shard_map/all_gather | solution.py:130
  147.5 82.1 %reduce-scatter.5.cloned.1.call-start = ((), (), s32[]{:S(2)}) async-start(), calls=%async_computation.5 | async-start | bytes 1966080 | tf_op jit(solution)/shard_map/reduce_scatter | solution.py:139
Sparse Core Ops, SparseCore 0:
  9.6 39.7 all-gather.6
  53.8 22.4 all-gather.10
  78.7 23.4 all-gather.12
  109.0 35.2 reduce-scatter.2
  147.6 36.0 all-gather.8
  195.4 34.1 reduce-scatter.4
where the time goes:
time: 237 us; the launch traced here: 236 us
  waiting for transfers between devices  181 us (76%)
  matrix products  31.5 us (13%)
  between operations  14.3 us (6%)
  other arithmetic  7.1 us (3%)
  local copies, waits for them, and re-layouts  2.62 us (1%)
    all_gather x1, waiting for transfers between devices, body(): lax.all_gather(residual_deposit_sequence, 'exp', axis=0, tiled=True)  41.4 us
    all_gather x1, waiting for transfers between devices, body(): rows = lax.all_gather(expert_in, 'exp', axis=0, tiled=True)  36 us
    reduce_scatter x1, waiting for transfers between devices, body(): lax.psum_scatter(partial_out.astype(jnp.bfloat16), 'exp', scatter_dimensi...  35.4 us
    reduce_scatter x1, waiting for transfers between devices, body(): lax.psum_scatter(summed.reshape(events, row_count, D), 'exp', scatter_dim...  34.3 us
    all_gather x1, waiting for transfers between devices, attend_hits(): value_piece = lax.all_gather(value_heads, 'blk', axis=1, tiled=True)  20.6 us
    all_gather x1, waiting for transfers between devices, attend_hits(): key_piece = lax.all_gather(key_heads, 'blk', axis=1, tiled=True)  12.2 us
    dot_general x1, matrix products, run_experts(): jnp.einsum('tjf,jfd->td', hidden, shrink, preferred_element_type=jnp.floa...  6.9 us
    dot_general x1, matrix products, attend_hits(): jnp.einsum('sikgd,sjkd->skgij', query_heads, key_piece, preferred_element...  5.4 us
  transfers between devices with their start and end apart: 6, of which 6 were waited for; matrix products, arithmetic and copies ran while one was open for 7% of the time, Pallas kernels for 0%

commit v1 on v0

--- a/solution.py
+++ b/solution.py
@@ -54,7 +54,12 @@
     inverse_root_dim = (logit_multipliers / math.sqrt(PER_LANE_DIM)).reshape(
         common_key_heads, askers_per_lookup
     )
-    key_piece = lax.all_gather(key_heads, "blk", axis=1, tiled=True)
+    ring = [key_heads]
+    for hop in range(7):
+        ring.append(lax.ppermute(ring[-1], "blk", [(dev, (dev + 1) % 8) for dev in range(8)]))
+    key_piece = jnp.roll(
+        jnp.concatenate(ring[::-1], axis=1), (lax.axis_index("blk") + 1) * ring[0].shape[1], axis=1
+    )
     value_piece = lax.all_gather(value_heads, "blk", axis=1, tiled=True)
     scores = jnp.einsum(
         "sikgd,sjkd->skgij", query_heads, key_piece, preferred_element_type=jnp.float32

time: 237 us -> 237 us (level)
  local copies, waits for them, and re-layouts: 2.62 us -> 9.25 us
  waiting for transfers between devices: 181 us -> 175 us
    ppermute x0 -> x7, waiting for transfers between devices: none -> 29.1 us  [attend_hits(): lax.ppermute(ring[-1], 'blk', [(dev, (dev + 1) % 8) for dev in range(8)])]
    all_gather x1, waiting for transfers between devices: 20.6 us -> 0.01 us  [attend_hits(): value_piece = lax.all_gather(value_heads, 'blk', axis=1, tiled=True)]
    all_gather x1 -> x0, waiting for transfers between devices: 12.2 us -> none  [attend_hits(): key_piece = lax.all_gather(key_heads, 'blk', axis=1, tiled=True)]
    unnamed x25 -> x45, local copies, waits for them, and re-layouts: 0.07 us -> 6.69 us
  transfers between devices with their start and end apart: 6 -> 12, of which waited for: 6 -> 10; matrix products, arithmetic and copies ran while one was open for 7% -> 9% of each run, Pallas kernels for 0% -> 0%
where the time goes in v1:
time: 237 us; the launch traced here: 236 us
  waiting for transfers between devices  175 us (74%)
  matrix products  30.5 us (13%)
  between operations  14.1 us (6%)
  local copies, waits for them, and re-layouts  9.25 us (4%)
  other arithmetic  6.76 us (3%)
    all_gather x1, waiting for transfers between devices, body(): lax.all_gather(residual_deposit_sequence, 'exp', axis=0, tiled=True)  41.4 us
    all_gather x1, waiting for transfers between devices, body(): rows = lax.all_gather(expert_in, 'exp', axis=0, tiled=True)  36 us
    reduce_scatter x1, waiting for transfers between devices, body(): lax.psum_scatter(summed.reshape(events, row_count, D), 'exp', scatter_dim...  34.3 us
    reduce_scatter x1, waiting for transfers between devices, body(): lax.psum_scatter(partial_out.astype(jnp.bfloat16), 'exp', scatter_dimensi...  33.4 us
    ppermute x7, waiting for transfers between devices, attend_hits(): lax.ppermute(ring[-1], 'blk', [(dev, (dev + 1) % 8) for dev in range(8)])  29.1 us
    dot_general x1, matrix products, run_experts(): jnp.einsum('tjf,jfd->td', hidden, shrink, preferred_element_type=jnp.floa...  6.91 us
    unnamed x45, local copies, waits for them, and re-layouts  6.69 us
  transfers between devices with their start and end apart: 12, of which 10 were waited for; matrix products, arithmetic and copies ran while one was open for 9% of the time, Pallas kernels for 0%

profile of v1, /device:TPU:0, one launch (start us, length us, event | category | flops | bytes accessed | tf_op | source)
XLA Modules:
  0.0 236.0 jit_solution(346614107656178426)
XLA Ops:
  7.2 0.0 copy-start
  7.2 0.0 all-gather.5.cloned.1.call-start
  7.2 0.7 all-gather.5.cloned.1.call-update
  7.9 0.0 all-gather.9.cloned.1.call-start
  8.0 41.4 %all-gather.5.cloned.1.call-done = bf16[4,128,1536]{2,1,0:T(8,128)(2,1)} async-done(((bf16[1,128,1536]{2,1,0:T(8,128)(2,1)}), bf16[4,128,1536]{2,1,0:T(8,128)(2,1)}) %all-gather.5.cloned.1.call-update) | async-done | bytes 1572880 | tf_op jit(solution)/shard_map/all_gather | solution.py:112
  49.4 1.8 fusion.1
  51.2 0.0 copy-start.12
  51.2 2.2 multiply_reduce_fusion.2
  53.5 0.1 fusion.26
  53.6 0.1 collective-permute-start
  53.7 5.3 %collective-permute-done = bf16[4,128,1,128]{3,1,0,2:T(8,128)(2,1)S(1)} collective-permute-done((bf16[4,128,1,128]{3,1,0,2:T(8,128)(2,1)S(1)}, bf16[4,128,1,128]{3,1,0,2:T(8,128)(2,1)S(1)}, u32[]{:S(2)}, u32[]{:S(2)}) %collective-permute-start) | collective-permute-done | bytes 131104 | tf_op jit(solution)/shard_map/ppermute | solution.py:59
  59.0 0.0 collective-permute-start.1
  59.0 5.3 %collective-permute-done.1 = bf16[4,128,1,128]{3,1,0,2:T(8,128)(2,1)S(1)} collective-permute-done((bf16[4,128,1,128]{3,1,0,2:T(8,128)(2,1)S(1)}, bf16[4,128,1,128]{3,1,0,2:T(8,128)(2,1)S(1)}, u32[]{:S(2)}, u32[]{:S(2)}) %collective-permute-start.1) | collective-permute-done | bytes 131104 | tf_op jit(solution)/shard_map/ppermute | solution.py:59
  64.3 0.0 collective-permute-start.2
  64.3 5.3 %collective-permute-done.2 = bf16[4,128,1,128]{3,1,0,2:T(8,128)(2,1)S(1)} collective-permute-done((bf16[4,128,1,128]{3,1,0,2:T(8,128)(2,1)S(1)}, bf16[4,128,1,128]{3,1,0,2:T(8,128)(2,1)S(1)}, u32[]{:S(2)}, u32[]{:S(2)}) %collective-permute-start.2) | collective-permute-done | bytes 131104 | tf_op jit(solution)/shard_map/ppermute | solution.py:59
  69.6 0.0 collective-permute-start.3
  69.6 0.0 copy-done.13
  69.6 0.1 dynamic-slice_multiply_fusion
  69.7 5.2 %collective-permute-done.3 = bf16[4,128,1,128]{3,1,0,2:T(8,128)(2,1)S(1)} collective-permute-done((bf16[4,128,1,128]{3,1,0,2:T(8,128)(2,1)S(1)}, bf16[4,128,1,128]{3,1,0,2:T(8,128)(2,1)S(1)}, u32[]{:S(2)}, u32[]{:S(2)}) %collective-permute-start.3) | collective-permute-done | bytes 131104 | tf_op jit(solution)/shard_map/ppermute | solution.py:59
  74.9 0.0 collective-permute-start.4
  74.9 0.0 copy-done.12
  74.9 2.7 %convolution_convert_fusion = bf16[4,128,128]{2,1,0:T(8,128)(2,1)} fusion(bf16[4,128,1536]{2,1,0:T(8,128)(2,1)} %all-gather.5.cloned.1.call-done, f32[1536]{0:T(1024)} %param.14, f32[4,128]{1,0:T(4,128)S(1)} %add_rsqrt_fusion.3, bf16[1536,128]{1,0:T(8,128)(2,1)S(1)} %copy-done.12), kind=kOutput, calls=%fused_computation.19 | convolution fusion | flops 204537856 | bytes 2105344 | tf_op jit(solution)/shard_map/std,de->ste/dot_general | solution.py:48
  77.6 0.0 all-gather.9.cloned.1.call-update
  77.6 0.0 reduce-scatter.3.cloned.1.call-start
  77.7 2.6 %collective-permute-done.4 = bf16[4,128,1,128]{3,1,0,2:T(8,128)(2,1)} collective-permute-done((bf16[4,128,1,128]{3,1,0,2:T(8,128)(2,1)S(1)}, bf16[4,128,1,128]{3,1,0,2:T(8,128)(2,1)}, u32[]{:S(2)}, u32[]{:S(2)}) %collective-permute-start.4) | collective-permute-done | bytes 131104 | tf_op jit(solution)/shard_map/ppermute | solution.py:59
  80.3 0.0 copy-done.4
  80.3 0.1 collective-permute-start.5
  80.3 3.7 %fusion.29 = (f32[4,128,384]{2,1,0:T(8,128)S(1)}, f32[4,128,384]{2,1,0:T(8,128)}) fusion(bf16[1536,384]{1,0:T(8,128)(2,1)} %param.15, bf16[4,128,1536]{2,1,0:T(8,128)(2,1)} %all-gather.5.cloned.1.call-done, f32[1536]{0:T(1024)} %param.14, f32[4,128]{1,0:T(4,128)S(1)} %add_rsqrt_fusion.3), kind=kOutput, calls=%fused_computation.68 | convolution fusion | flops 607322112 | bytes 4333568 | tf_op jit(solution)/shard_map/std,de->ste/dot_general | solution.py:36
  84.0 1.2 copy.36
  85.2 1.4 copy.35
  86.6 1.2 reduce_sum.65
  87.8 0.0 copy-start.7
  87.8 0.0 copy-start.5
  87.8 0.0 collective-permute-done.5
  87.8 0.1 collective-permute-start.6
  87.9 5.5 %collective-permute-done.6 = bf16[4,128,1,128]{3,1,0,2:T(8,128)(2,1)S(1)} collective-permute-done((bf16[4,128,1,128]{3,1,0,2:T(8,128)(2,1)}, bf16[4,128,1,128]{3,1,0,2:T(8,128)(2,1)S(1)}, u32[]{:S(2)}, u32[]{:S(2)}) %collective-permute-start.6) | collective-permute-done | bytes 131104 | tf_op jit(solution)/shard_map/ppermute | solution.py:59
  93.4 0.9 constant_dynamic-update-slice_fusion.14
  94.3 0.9 constant_dynamic-update-slice_fusion.13
  95.2 0.9 constant_dynamic-update-slice_fusion.12
  96.2 0.9 constant_dynamic-update-slice_fusion.11
  97.1 0.9 constant_dynamic-update-slice_fusion.10
  98.0 0.2 constant_dynamic-update-slice_fusion.8
  98.2 0.9 constant_dynamic-update-slice_fusion.6
  99.2 0.9 constant_dynamic-update-slice_fusion.5
  100.2 0.0 copy-done.3
  100.2 0.2 constant_dynamic-update-slice_fusion
  100.4 3.7 %bitcast_reduce_fusion = (f32[4,3,128]{2,1,0:T(4,128)S(1)}, f32[4,1024,128,3]{2,1,3,0:T(8,128)}) fusion(f32[3]{0:T(128)S(1)} %dynamic-slice_multiply_fusion, f32[4,128,3,128]{1,3,2,0:T(8,128)S(1)} %bitcast.90, f32[4,128,3]{1,2,0:T(4,128)S(1)} %add_rsqrt_fusion.1, bf16[4,2048,1,128]{3,1,0,2:T(8,128)(2,1)S(1)} %constant_dynamic-update-slice_fusion, s32[]{:T(128)S(6)} %select_n.21), kind=kOutput, calls=%fused_computation | convolution fusion | flops 406190592 | bytes 8141316 | tf_op jit(solution)/shard_map/sikgd,sjkd->skgij/dot_general | solution.py:64
  104.1 4.4 %multiply_reduce_fusion.1 = (f32[4,3,128]{2,1,0:T(4,128)S(1)}, f32[4,3,128,128]{2,3,1,0:T(8,128)S(1)}) fusion(f32[4,3,128]{2,1,0:T(4,128)S(1)} %get-tuple-element.6, bf16[4,1024,128]{2,1,0:T(8,128)(2,1)} %all-gather.9.cloned.1.call-done, f32[4,1024,128,3]{2,1,3,0:T(8,128)} %get-tuple-element.7, f32[3]{0:T(128)S(1)} %dynamic-slice_multiply_fusion), kind=kOutput, calls=%fused_computation.31 | convolution fusion | flops 406387200 | bytes 8138764 | tf_op jit(solution)/shard_map/skgij,sjkd->skgid/dot_general | solution.py:69
  108.5 0.0 copy-start.1
  108.5 2.2 fusion.8
  110.7 0.0 reduce-scatter.3.cloned.1.call-update
  110.8 0.0 all-gather.7.cloned.1.call-start
  110.8 33.4 %reduce-scatter.3.cloned.1.call-done = bf16[1,128,1536]{2,1,0:T(8,128)(2,1)} async-done(((bf16[4,128,1536]{2,1,0:T(8,128)(2,1)}), bf16[1,128,1536]{2,1,0:T(8,128)(2,1)}) %reduce-scatter.3.cloned.1.call-update) | async-done | bytes 393232 | tf_op jit(solution)/shard_map/reduce_scatter | solution.py:126
  144.2 1.2 multiply_reduce_fusion
  145.4 0.0 copy-done.8
  145.4 1.9 multiply_convert_fusion.1
  147.3 0.0 all-gather.7.cloned.1.call-update
  147.3 0.0 reduce-scatter.5.cloned.1.call-start
  147.4 0.1 select_reduce_fusion
  147.5 36.0 %all-gather.7.cloned.1.call-done = bf16[4,128,1536]{2,1,0:T(8,128)(2,1)} async-done(((bf16[1,128,1536]{2,1,0:T(8,128)(2,1)}), bf16[4,128,1536]{2,1,0:T(8,128)(2,1)}) %all-gather.7.cloned.1.call-update) | async-done | bytes 1572880 | tf_op jit(solution)/shard_map/all_gather | solution.py:135
  183.6 4.7 %fusion.30 = f32[512,2,384]{2,0,1:T(8,128)} fusion(bf16[512,1536,1]{1,0,2:T(8,128)(2,1)} %bitcast.95, bf16[2,1536,384]{2,1,0:T(8,128)(2,1)} %param.21), kind=kOutput, calls=%fused_computation.69 | convolution fusion | flops 1207959552 | bytes 5505024 | tf_op jit(solution)/shard_map/td,jdf->tjf/dot_general | solution.py:89
  188.2 6.9 %fusion.9 = bf16[512,1536]{1,0:T(8,128)(2,1)} fusion(bf16[2,384,1536]{2,1,0:T(8,128)(2,1)S(1)} %copy-done, f32[512,2,384]{2,0,1:T(8,128)} %fusion.30, bf16[512,1536,1]{1,0,2:T(8,128)(2,1)} %bitcast.96, bf16[2,1536,384]{2,1,0:T(8,128)(2,1)} %param.22, f32[512,2]{0,1:T(2,128)S(1)} %bitcast.94), kind=kOutput, calls=%fused_computation.15 | convolution fusion | flops 2419458048 | bytes 9441280 | tf_op jit(solution)/shard_map/tjf,jfd->td/dot_general | solution.py:92
  195.1 0.0 reduce-scatter.5.cloned.1.call-update
  195.2 34.3 %reduce-scatter.5.cloned.1.call-done = bf16[1,128,1536]{2,1,0:T(8,128)(2,1)} async-done(((bf16[4,128,1536]{2,1,0:T(8,128)(2,1)}), bf16[1,128,1536]{2,1,0:T(8,128)(2,1)}) %reduce-scatter.5.cloned.1.call-update) | async-done | bytes 393232 | tf_op jit(solution)/shard_map/reduce_scatter | solution.py:144
  (35 shorter events, 0.2 us)
Async XLA Ops:
  7.2 181.1 %copy-start = (bf16[2,384,1536]{2,1,0:T(8,128)(2,1)S(1)}, bf16[2,384,1536]{2,1,0:T(8,128)(2,1)}, u32[]{:S(2)}) copy-start(bf16[2,384,1536]{2,1,0:T(8,128)(2,1)} %param.23) | copy-start | bytes 7077892
  7.2 42.2 %all-gather.5.cloned.1.call-start = ((), (), s32[]{:S(2)}) async-start(), calls=%async_computation.2 | async-start | bytes 1966080 | tf_op jit(solution)/shard_map/all_gather | solution.py:112
  7.9 96.2 %all-gather.9.cloned.1.call-start = ((), (), s32[]{:S(2)}) async-start(), calls=%async_computation.6 | async-start | bytes 1179648 | tf_op jit(solution)/shard_map/all_gather | solution.py:63
  51.2 18.4 %copy-start.13 = (f32[12]{0:T(128)S(1)}, f32[12]{0:T(128)}, u32[]{:S(2)}) copy-start(f32[12]{0:T(128)} %param.19) | copy-start | bytes 148
  51.2 23.7 %copy-start.12 = (bf16[1536,128]{1,0:T(8,128)(2,1)S(1)}, bf16[1536,128]{1,0:T(8,128)(2,1)}, u32[]{:S(2)}) copy-start(bf16[1536,128]{1,0:T(8,128)(2,1)} %param.17) | copy-start | bytes 1179652
  53.6 5.3 %collective-permute-start = (bf16[4,128,1,128]{3,1,0,2:T(8,128)(2,1)S(1)}, bf16[4,128,1,128]{3,1,0,2:T(8,128)(2,1)S(1)}, u32[]{:S(2)}, u32[]{:S(2)}) collective-permute-start(bf16[4,128,1,128]{3,1,0,2:T(8,128)(2,1)S(1)} %fusion.26), channel_id=1, source_target_pairs={{0,4},{4,8},{8,12},{12,16},{16,20},{20,24},{24,28},{28,0},{1,5},{5... | collective-permute-start | bytes 393224 | tf_op jit(solution)/shard_map/ppermute | solution.py:59
  59.0 5.3 %collective-permute-start.1 = (bf16[4,128,1,128]{3,1,0,2:T(8,128)(2,1)S(1)}, bf16[4,128,1,128]{3,1,0,2:T(8,128)(2,1)S(1)}, u32[]{:S(2)}, u32[]{:S(2)}) collective-permute-start(bf16[4,128,1,128]{3,1,0,2:T(8,128)(2,1)S(1)} %collective-permute-done), channel_id=1, source_target_pairs={{0,4},{4,8},{8,12},{12,16},{16,20},{20,24},{24,28},{28,0},{1,5},{5... | collective-permute-start | bytes 393224 | tf_op jit(solution)/shard_map/ppermute | solution.py:59
  64.3 16.0 %copy-start.2 = (bf16[4,128,1,128]{3,1,0,2:T(8,128)(2,1)}, bf16[4,128,1,128]{3,1,0,2:T(8,128)(2,1)S(1)}, u32[]{:S(2)}) copy-start(bf16[4,128,1,128]{3,1,0,2:T(8,128)(2,1)S(1)} %collective-permute-done.1) | copy-start | bytes 393220
  64.3 5.3 %collective-permute-start.2 = (bf16[4,128,1,128]{3,1,0,2:T(8,128)(2,1)S(1)}, bf16[4,128,1,128]{3,1,0,2:T(8,128)(2,1)S(1)}, u32[]{:S(2)}, u32[]{:S(2)}) collective-permute-start(bf16[4,128,1,128]{3,1,0,2:T(8,128)(2,1)S(1)} %collective-permute-done.1), channel_id=1, source_target_pairs={{0,4},{4,8},{8,12},{12,16},{16,20},{20,24},{24,28},{28,0},{1,5},{5... | collective-permute-start | bytes 393224 | tf_op jit(solution)/shard_map/ppermute | solution.py:59
  69.6 10.7 %copy-start.4 = (bf16[4,128,1,128]{3,1,0,2:T(8,128)(2,1)}, bf16[4,128,1,128]{3,1,0,2:T(8,128)(2,1)S(1)}, u32[]{:S(2)}) copy-start(bf16[4,128,1,128]{3,1,0,2:T(8,128)(2,1)S(1)} %collective-permute-done.2) | copy-start | bytes 393220
  69.6 5.3 %collective-permute-start.3 = (bf16[4,128,1,128]{3,1,0,2:T(8,128)(2,1)S(1)}, bf16[4,128,1,128]{3,1,0,2:T(8,128)(2,1)S(1)}, u32[]{:S(2)}, u32[]{:S(2)}) collective-permute-start(bf16[4,128,1,128]{3,1,0,2:T(8,128)(2,1)S(1)} %collective-permute-done.2), channel_id=1, source_target_pairs={{0,4},{4,8},{8,12},{12,16},{16,20},{20,24},{24,28},{28,0},{1,5},{5... | collective-permute-start | bytes 393224 | tf_op jit(solution)/shard_map/ppermute | solution.py:59
  74.9 5.4 %copy-start.6 = (bf16[4,128,1,128]{3,1,0,2:T(8,128)(2,1)}, bf16[4,128,1,128]{3,1,0,2:T(8,128)(2,1)S(1)}, u32[]{:S(2)}) copy-start(bf16[4,128,1,128]{3,1,0,2:T(8,128)(2,1)S(1)} %collective-permute-done.3) | copy-start | bytes 393220
  74.9 5.4 %collective-permute-start.4 = (bf16[4,128,1,128]{3,1,0,2:T(8,128)(2,1)S(1)}, bf16[4,128,1,128]{3,1,0,2:T(8,128)(2,1)}, u32[]{:S(2)}, u32[]{:S(2)}) collective-permute-start(bf16[4,128,1,128]{3,1,0,2:T(8,128)(2,1)S(1)} %collective-permute-done.3), channel_id=1, source_target_pairs={{0,4},{4,8},{8,12},{12,16},{16,20},{20,24},{24,28},{28,0},{1,5},{5... | collective-permute-start | bytes 393224 | tf_op jit(solution)/shard_map/ppermute | solution.py:59
  77.6 66.5 %reduce-scatter.3.cloned.1.call-start = ((), (), s32[]{:S(2)}) async-start(), calls=%async_computation.3 | async-start | bytes 1966080 | tf_op jit(solution)/shard_map/reduce_scatter | solution.py:126
  80.3 7.5 %collective-permute-start.5 = (bf16[4,128,1,128]{3,1,0,2:T(8,128)(2,1)}, bf16[4,128,1,128]{3,1,0,2:T(8,128)(2,1)}, u32[]{:S(2)}, u32[]{:S(2)}) collective-permute-start(bf16[4,128,1,128]{3,1,0,2:T(8,128)(2,1)} %collective-permute-done.4), channel_id=1, source_target_pairs={{0,4},{4,8},{8,12},{12,16},{16,20},{20,24},{24,28},{28,0},{1,5},{5... | collective-permute-start | bytes 393224 | tf_op jit(solution)/shard_map/ppermute | solution.py:59
  87.8 12.3 %copy-start.7 = (bf16[4,128,1,128]{3,1,0,2:T(8,128)(2,1)S(1)}, bf16[4,128,1,128]{3,1,0,2:T(8,128)(2,1)}, u32[]{:S(2)}) copy-start(bf16[4,128,1,128]{3,1,0,2:T(8,128)(2,1)} %copy-done.6) | copy-start | bytes 393220
  87.8 12.4 %copy-start.5 = (bf16[4,128,1,128]{3,1,0,2:T(8,128)(2,1)S(1)}, bf16[4,128,1,128]{3,1,0,2:T(8,128)(2,1)}, u32[]{:S(2)}) copy-start(bf16[4,128,1,128]{3,1,0,2:T(8,128)(2,1)} %copy-done.4) | copy-start | bytes 393220
  87.8 12.4 %copy-start.3 = (bf16[4,128,1,128]{3,1,0,2:T(8,128)(2,1)S(1)}, bf16[4,128,1,128]{3,1,0,2:T(8,128)(2,1)}, u32[]{:S(2)}) copy-start(bf16[4,128,1,128]{3,1,0,2:T(8,128)(2,1)} %copy-done.2) | copy-start | bytes 393220
  87.8 5.6 %collective-permute-start.6 = (bf16[4,128,1,128]{3,1,0,2:T(8,128)(2,1)}, bf16[4,128,1,128]{3,1,0,2:T(8,128)(2,1)S(1)}, u32[]{:S(2)}, u32[]{:S(2)}) collective-permute-start(bf16[4,128,1,128]{3,1,0,2:T(8,128)(2,1)} %collective-permute-done.5), channel_id=1, source_target_pairs={{0,4},{4,8},{8,12},{12,16},{16,20},{20,24},{24,28},{28,0},{1,5},{5... | collective-permute-start | bytes 393224 | tf_op jit(solution)/shard_map/ppermute | solution.py:59
  104.1 4.5 %copy-start.11 = (bf16[384,1536]{1,0:T(8,128)(2,1)S(1)}, bf16[384,1536]{1,0:T(8,128)(2,1)}, u32[]{:S(2)}) copy-start(bf16[384,1536]{1,0:T(8,128)(2,1)} %param.18) | copy-start | bytes 3538948
  108.5 35.7 %copy-start.1 = (bf16[1,128,1536]{2,1,0:T(8,128)(2,1)S(1)}, bf16[1,128,1536]{2,1,0:T(8,128)(2,1)}, u32[]{:S(2)}) copy-start(bf16[1,128,1536]{2,1,0:T(8,128)(2,1)} %param.13) | copy-start | bytes 1179652
  110.7 34.7 %copy-start.8 = (f32[1536]{0:T(1024)S(1)}, f32[1536]{0:T(1024)}, u32[]{:S(2)}) copy-start(f32[1536]{0:T(1024)} %param.20) | copy-start | bytes 18436
  110.7 36.7 %copy-start.9 = (s32[4,128,2]{1,2,0:T(2,128)S(1)}, s32[4,128,2]{1,2,0:T(2,128)}, u32[]{:S(2)}) copy-start(s32[4,128,2]{1,2,0:T(2,128)} %param.24) | copy-start | bytes 12292
  110.7 36.7 %copy-start.10 = (f32[4,128,2]{1,2,0:T(2,128)S(1)}, f32[4,128,2]{1,2,0:T(2,128)}, u32[]{:S(2)}) copy-start(f32[4,128,2]{1,2,0:T(2,128)} %param.25) | copy-start | bytes 12292
  110.8 72.8 %all-gather.7.cloned.1.call-start = ((), (), s32[]{:S(2)}) async-start(), calls=%async_computation.4 | async-start | bytes 1966080 | tf_op jit(solution)/shard_map/all_gather | solution.py:135
  147.3 82.2 %reduce-scatter.5.cloned.1.call-start = ((), (), s32[]{:S(2)}) async-start(), calls=%async_computation.5 | async-start | bytes 1966080 | tf_op jit(solution)/shard_map/reduce_scatter | solution.py:144
Sparse Core Ops, SparseCore 0:
  9.6 39.7 all-gather.4
  77.8 22.9 all-gather.8
  110.9 33.2 reduce-scatter.2
  147.4 36.0 all-gather.6
  195.3 34.1 reduce-scatter.4
